TPU v7x, 32 devices: a whole 2x2x4 slice. The times are simulated.
32 devices in a mesh: row: 2 (over y), col: 8 (over z, core), depth: 2 (over x).
Axes of the slice: x: 2, y: 2, z: 4, core: 2. Of those that a mesh axis runs over, the one named last changes fastest.
Arguments:
- cube: bfloat16 [512, 512, 512], P('row', 'col', 'depth'), may hold values from -18 to 18
- mode3_factor: bfloat16 [512, 256], P('depth'), may hold values from -0.375 to 0.375
- mode2_factor: bfloat16 [512, 256], P('col'), may hold values from -0.375 to 0.375
- start_basis: float32 [512, 256], P('row'), may hold values from -6 to 6
Outputs:
- factor: float32 [512, 256], P('row')
All inputs are finite; a program needn't handle non-finite values.
Results may differ from a plain program's by a relative error of at most 0.023.
Values may be sent and summed in bfloat16 or wider, within the bound.
A program may use at most 128 MiB of HBM per device.

v0:
```python
import math

import jax
import jax.numpy as jnp
from jax import lax
from jax.sharding import PartitionSpec as P

I1 = 512
ITERS = 4


def orthonormal(image, cross):
    lower = jnp.linalg.cholesky(cross)
    return jax.scipy.linalg.solve_triangular(lower, image.T, lower=True).T


def shards(cube, mode3_factor, mode2_factor, start_basis):
    rows, width2, width3 = cube.shape
    rank = mode3_factor.shape[1]
    n_depth = lax.axis_size("depth")
    n_col = lax.axis_size("col")
    flat = cube.reshape(rows * width2, width3)
    rank3 = rank // n_depth
    columns = mode3_factor
    middle = lax.psum_scatter(
        lax.dot_general(
            columns, flat, (((0,), (1,)), ((), ())), preferred_element_type=jnp.float32
        ).astype(jnp.bfloat16),
        "depth",
        scatter_dimension=0,
        tiled=True,
    )
    middle = middle.reshape(rank3, rows, width2)
    rank2 = rank // n_col
    columns = mode2_factor
    product = jnp.einsum("tij,jr->rti", middle, columns, preferred_element_type=jnp.float32)
    core = lax.psum_scatter(
        product.reshape(rank2 * lax.axis_size("col"), rank3 * rows).astype(jnp.bfloat16),
        "col",
        scatter_dimension=0,
        tiled=True,
    )
    core = core.reshape(rank2 * rank3, rows)
    partial_gram = lax.dot_general(
        core,
        lax.all_gather(core, "row", axis=1, tiled=True),
        (((0,), (0,)), ((), ())),
        preferred_element_type=jnp.float32,
    )
    gram_rows = lax.psum(partial_gram, ("col", "depth"))
    gram, basis = (
        lax.all_gather(gram_rows, "row", axis=0, tiled=True),
        lax.all_gather(start_basis, "row", axis=0, tiled=True),
    )
    for step in range(ITERS):
        image = jnp.dot(gram, basis, precision=lax.Precision.HIGHEST)
        cross = lax.dot_general(
            image, image, (((0,), (0,)), ((), ())), precision=lax.Precision.HIGHEST
        )
        basis = orthonormal(image, cross)
    basis = lax.dynamic_slice_in_dim(basis, lax.axis_index("row") * rows, rows, 0)
    return basis * math.sqrt(I1)


def solution(mesh):
    in_specs = (P("row", "col", "depth"), P("depth", None), P("col", None), P("row", None))
    out_specs = P("row", None)
    return jax.shard_map(shards, mesh=mesh, in_specs=in_specs, out_specs=out_specs, check_vma=False)
```

profile of v0, /device:TPU:0, one launch (start us, length us, event | category | flops | bytes accessed | tf_op | source)
XLA Modules:
  0.0 777.7 jit_solution(8187777402938403174)
XLA Ops:
  16.5 102.0 %reduce-scatter.3.cloned.1.call-done = bf16[128,16384]{1,0:T(8,128)(2,1)} async-done(((bf16[256,16384]{1,0:T(8,128)(2,1)}), bf16[128,16384]{1,0:T(8,128)(2,1)}) %reduce-scatter.3.cloned.1.call-update) | async-done | bytes 4194320 | tf_op jit(solution)/shard_map/reduce_scatter | solution.py:25
  132.3 12.5 %convolution_convert_fusion.1 = bf16[128,256,256]{2,1,0:T(8,128)(2,1)} fusion(bf16[128,256,64]{1,2,0:T(8,128)(2,1)} %copy.12, bf16[64,256]{1,0:T(8,128)(2,1)S(1)} %copy-done.4), kind=kOutput, calls=%fused_computation.9 | convolution fusion | flops 1082130432 | bytes 21004288 | tf_op jit(solution)/shard_map/tij,jr->rti/dot_general | solution.py:36
  144.8 21.2 %copy.13 = bf16[256,32768]{1,0:T(8,128)(2,1)} copy(bf16[256,32768]{0,1:T(8,128)(2,1)} %bitcast.156) | data formatting | bytes 33554432 | tf_op jit(solution)/shard_map/convert_element_type | solution.py:38
  166.1 168.4 %reduce-scatter.5.cloned.1.call-done = bf16[32,32768]{1,0:T(8,128)(2,1)} async-done(((bf16[256,32768]{1,0:T(8,128)(2,1)}), bf16[32,32768]{1,0:T(8,128)(2,1)}) %reduce-scatter.5.cloned.1.call-update) | async-done | bytes 2097168 | tf_op jit(solution)/shard_map/reduce_scatter | solution.py:37
  338.8 55.2 %all-gather.3.cloned.1.call-done = bf16[4096,512]{1,0:T(8,128)(2,1)} async-done(((bf16[4096,256]{1,0:T(8,128)(2,1)}), bf16[4096,512]{1,0:T(8,128)(2,1)}) %all-gather.3.cloned.1.call-update) | async-done | bytes 4194320 | tf_op jit(solution)/shard_map/all_gather | solution.py:46
  398.9 90.2 %all-reduce.3.cloned.1.call-done = f32[256,512]{1,0:T(8,128)} async-done(((f32[256,512]{1,0:T(8,128)}), f32[256,512]{1,0:T(8,128)}) %all-reduce.3.cloned.1.call-update) | async-done | bytes 524304 | tf_op jit(solution)/shard_map/psum | solution.py:50
  489.2 9.8 %all_gather.11 = f32[512,256]{1,0:T(8,128)S(1)} all-gather(f32[256,256]{1,0:T(8,128)S(1)} %copy-done.3), channel_id=1, replica_groups=mesh['row'=2,'col'=8,'depth'=2] {'row'}, dimensions={0}, use_global_device_ids=true | all-gather | bytes 786432 | tf_op jit(solution)/shard_map/all_gather | solution.py:53
  499.0 13.4 %all-gather.5.cloned.1.call-done = f32[512,512]{1,0:T(8,128)} async-done(((f32[256,512]{1,0:T(8,128)}), f32[512,512]{1,0:T(8,128)}) %all-gather.5.cloned.1.call-update) | async-done | bytes 1048592 | tf_op jit(solution)/shard_map/all_gather | solution.py:52
  515.9 11.7 %cholesky.214 = f32[128,128]{1,0:T(8,128)S(1)} custom-call(f32[128,128]{1,0:T(8,128)S(1)} %cholesky.346), custom_call_target="Cholesky" | custom-call | tf_op jit(solution)/shard_map/jit(cholesky)/cholesky | solution.py:13
  527.6 9.8 %custom-call.17 = f32[1,128,128]{1,2,0:T(8,128)S(1)} custom-call(f32[1,128,128]{2,1,0:T(8,128)S(1)} %get-tuple-element.92), custom_call_target="InvertDiagBlocksLowerTriangular" | custom-call | tf_op jit(solution)/shard_map/jit(cholesky)/cholesky | solution.py:13
  537.9 11.9 %cholesky.231 = f32[128,128]{1,0:T(8,128)S(1)} custom-call(f32[128,128]{1,0:T(8,128)S(1)} %convolution_subtract_fusion.7), custom_call_target="Cholesky" | custom-call | tf_op jit(solution)/shard_map/jit(cholesky)/cholesky | solution.py:13
  556.0 19.7 %custom-call.18 = f32[2,128,128]{1,2,0:T(8,128)S(1)} custom-call(f32[2,128,128]{2,1,0:T(8,128)S(1)} %get-tuple-element.33), custom_call_target="InvertDiagBlocksLowerTriangular" | custom-call | tf_op jit(solution)/shard_map/jit(_solve_triangular)/triangular_solve | solution.py:14
  579.4 11.7 %cholesky.248 = f32[128,128]{1,0:T(8,128)S(1)} custom-call(f32[128,128]{1,0:T(8,128)S(1)} %cholesky.349), custom_call_target="Cholesky" | custom-call | tf_op jit(solution)/shard_map/jit(cholesky)/cholesky | solution.py:13
  591.2 9.8 %custom-call.19 = f32[1,128,128]{1,2,0:T(8,128)S(1)} custom-call(f32[1,128,128]{2,1,0:T(8,128)S(1)} %get-tuple-element.88), custom_call_target="InvertDiagBlocksLowerTriangular" | custom-call | tf_op jit(solution)/shard_map/jit(cholesky)/cholesky | solution.py:13
  601.5 12.1 %cholesky.265 = f32[128,128]{1,0:T(8,128)S(1)} custom-call(f32[128,128]{1,0:T(8,128)S(1)} %convolution_subtract_fusion.6), custom_call_target="Cholesky" | custom-call | tf_op jit(solution)/shard_map/jit(cholesky)/cholesky | solution.py:13
  620.5 19.7 %custom-call.20 = f32[2,128,128]{1,2,0:T(8,128)S(1)} custom-call(f32[2,128,128]{2,1,0:T(8,128)S(1)} %get-tuple-element.34), custom_call_target="InvertDiagBlocksLowerTriangular" | custom-call | tf_op jit(solution)/shard_map/jit(_solve_triangular)/triangular_solve | solution.py:14
  643.9 11.7 %cholesky.282 = f32[128,128]{1,0:T(8,128)S(1)} custom-call(f32[128,128]{1,0:T(8,128)S(1)} %cholesky.352), custom_call_target="Cholesky" | custom-call | tf_op jit(solution)/shard_map/jit(cholesky)/cholesky | solution.py:13
  655.6 9.8 %custom-call.21 = f32[1,128,128]{1,2,0:T(8,128)S(1)} custom-call(f32[1,128,128]{2,1,0:T(8,128)S(1)} %get-tuple-element.84), custom_call_target="InvertDiagBlocksLowerTriangular" | custom-call | tf_op jit(solution)/shard_map/jit(cholesky)/cholesky | solution.py:13
  665.9 11.9 %cholesky.299 = f32[128,128]{1,0:T(8,128)S(1)} custom-call(f32[128,128]{1,0:T(8,128)S(1)} %convolution_subtract_fusion.5), custom_call_target="Cholesky" | custom-call | tf_op jit(solution)/shard_map/jit(cholesky)/cholesky | solution.py:13
  684.7 19.7 %custom-call.22 = f32[2,128,128]{1,2,0:T(8,128)S(1)} custom-call(f32[2,128,128]{2,1,0:T(8,128)S(1)} %get-tuple-element.35), custom_call_target="InvertDiagBlocksLowerTriangular" | custom-call | tf_op jit(solution)/shard_map/jit(_solve_triangular)/triangular_solve | solution.py:14
  708.1 11.7 %cholesky.316 = f32[128,128]{1,0:T(8,128)S(1)} custom-call(f32[128,128]{1,0:T(8,128)S(1)} %cholesky.355), custom_call_target="Cholesky" | custom-call | tf_op jit(solution)/shard_map/jit(cholesky)/cholesky | solution.py:13
  719.9 9.8 %custom-call.23 = f32[1,128,128]{1,2,0:T(8,128)S(1)} custom-call(f32[1,128,128]{2,1,0:T(8,128)S(1)} %get-tuple-element.80), custom_call_target="InvertDiagBlocksLowerTriangular" | custom-call | tf_op jit(solution)/shard_map/jit(cholesky)/cholesky | solution.py:13
  730.2 11.9 %cholesky.333 = f32[128,128]{1,0:T(8,128)S(1)} custom-call(f32[128,128]{1,0:T(8,128)S(1)} %convolution_subtract_fusion.4), custom_call_target="Cholesky" | custom-call | tf_op jit(solution)/shard_map/jit(cholesky)/cholesky | solution.py:13
  749.0 19.7 %custom-call.24 = f32[2,128,128]{1,2,0:T(8,128)S(1)} custom-call(f32[2,128,128]{2,1,0:T(8,128)S(1)} %get-tuple-element.36), custom_call_target="InvertDiagBlocksLowerTriangular" | custom-call | tf_op jit(solution)/shard_map/jit(_solve_triangular)/triangular_solve | solution.py:14
  (124 shorter events, 89.5 us)
Async XLA Ops:
  6.5 0.9 copy-start
  6.5 112.0 %reduce-scatter.3.cloned.1.call-start = ((), (), s32[]{:S(2)}) async-start(), calls=%async_computation.2 | async-start | bytes 12582912 | tf_op jit(solution)/shard_map/reduce_scatter | solution.py:25
  16.5 318.0 %reduce-scatter.5.cloned.1.call-start = ((), (), s32[]{:S(2)}) async-start(), calls=%async_computation.3 | async-start | bytes 18874368 | tf_op jit(solution)/shard_map/reduce_scatter | solution.py:37
  125.0 7.4 copy-start.4
  166.0 227.9 %all-gather.3.cloned.1.call-start = ((), (), s32[]{:S(2)}) async-start(), calls=%async_computation.4 | async-start | bytes 6291456 | tf_op jit(solution)/shard_map/all_gather | solution.py:46
  338.7 150.5 %copy-start.3 = (f32[256,256]{1,0:T(8,128)S(1)}, f32[256,256]{1,0:T(8,128)}, u32[]{:S(2)}) copy-start(f32[256,256]{1,0:T(8,128)} %param.10) | copy-start | bytes 786436
  338.7 150.4 %all-reduce.3.cloned.1.call-start = ((), (), s32[]{:S(2)}) async-start(), calls=%async_computation.5 | async-start | bytes 1048576 | tf_op jit(solution)/shard_map/psum | solution.py:50
  398.8 113.6 %all-gather.5.cloned.1.call-start = ((), (), s32[]{:S(2)}) async-start(), calls=%async_computation.6 | async-start | bytes 1572864 | tf_op jit(solution)/shard_map/all_gather | solution.py:52
  514.6 62.5 %copy-start.2 = (f32[512,512]{1,0:T(8,128)S(1)}, f32[512,512]{1,0:T(8,128)}, u32[]{:S(2)}) copy-start(f32[512,512]{1,0:T(8,128)} %all-gather.5.cloned.1.call-done) | copy-start | bytes 3145732
  705.8 65.1 %copy-start.1 = (bf16[256,256]{1,0:T(8,128)(2,1)S(1)}, bf16[256,256]{1,0:T(8,128)(2,1)}, u32[]{:S(2)}) copy-start(bf16[256,256]{1,0:T(8,128)(2,1)} %param.8) | copy-start | bytes 393220
Sparse Core Ops, SparseCore 0:
  16.6 101.9 reduce-scatter.2
  166.2 168.2 reduce-scatter.4
  338.8 55.0 all-gather.2
  399.0 90.1 all-reduce.2
  490.6 21.7 all-gather.4
where the time goes:
time: 786 us; the launch traced here: 778 us
  waiting for transfers between devices  429 us (55%)
  other arithmetic  218 us (28%)
  local copies, waits for them, and re-layouts  57.9 us (7%)
  matrix products  43.3 us (6%)
  between operations  19.2 us (2%)
  blocking collectives  9.81 us (1%)
    reduce_scatter x1, waiting for transfers between devices, shards(): lax.psum_scatter(product.reshape(rank2 * lax.axis_size('col'), rank3 * ro...  168 us
    another operation x27, other arithmetic, orthonormal(): lower = jnp.linalg.cholesky(cross)  139 us
    reduce_scatter x1, waiting for transfers between devices, shards(): lax.psum_scatter(lax.dot_general(columns, flat, (((0,), (1,)), ((), ())),...  102 us
    psum x1, waiting for transfers between devices, shards(): gram_rows = lax.psum(partial_gram, ('col', 'depth'))  90.2 us
    another operation x9, other arithmetic, orthonormal(): return jax.scipy.linalg.solve_triangular(lower, image.T, lower=True).T  78.8 us
    all_gather x1, waiting for transfers between devices, shards(): lax.all_gather(core, 'row', axis=1, tiled=True)  55.2 us
    convert_element_type x1, local copies, waits for them, and re-layouts, shards(): product.reshape(rank2 * lax.axis_size('col'), rank3 * rows)  21.2 us
    another operation x29, local copies, waits for them, and re-layouts, orthonormal(): return jax.scipy.linalg.solve_triangular(lower, image.T, lower=True).T  16.3 us
  transfers between devices with their start and end apart: 5, of which 5 were waited for; matrix products, arithmetic and copies ran while one was open for 0% of the time, Pallas kernels for 0%

commit v1 on v0

v1 whole, which is shorter than its diff:
```python
import functools
import math

import jax
import jax.numpy as jnp
from jax import lax
from jax.experimental import pallas as pl
from jax.experimental.pallas import tpu as pltpu
from jax.sharding import PartitionSpec as P

ITERS = 4
OUTER = 64
HIGHEST = lax.Precision.HIGHEST


def dot(a, b, ca, cb, precision=HIGHEST):
    return lax.dot_general(
        a, b, (((ca,), (cb,)), ((), ())), precision=precision, preferred_element_type=jnp.float32
    )


def block_inverse(block):
    n = OUTER
    lane = lax.broadcasted_iota(jnp.int32, (n, n), 1)
    sub = lax.broadcasted_iota(jnp.int32, (n, n), 0)
    eye = jnp.where(lane == sub, 1.0, 0.0).astype(jnp.float32)
    whole = jnp.concatenate([block, eye], axis=1)
    tiles = [whole[8 * v : 8 * v + 8, :] for v in range(n // 8)]
    sublane = lax.broadcasted_iota(jnp.int32, (8, 2 * n), 0)
    full = (8, 2 * n)
    for b in range(n // 8):
        tile = tiles[b]
        d = {}
        for j in range(8):
            column = jnp.broadcast_to(tile[:, 8 * b + j : 8 * b + j + 1], full)
            for i in range(j, 8):
                d[i, j] = jnp.broadcast_to(column[i : i + 1, :], full)
        rows = [jnp.broadcast_to(tile[k : k + 1, :], full) for k in range(8)]
        low, p, reduced = {}, [], []
        for j in range(8):
            p.append(lax.rsqrt(d[j, j]))
            for i in range(j + 1, 8):
                low[i, j] = d[i, j] * p[j]
            for k in range(j + 1, 8):
                for i in range(k, 8):
                    d[i, k] = d[i, k] - low[i, j] * low[k, j]
            row = rows[j] * p[j]
            reduced.append(row)
            for i in range(j + 1, 8):
                rows[i] = rows[i] - low[i, j] * row
        out = reduced[0]
        for k in range(1, 8):
            out = jnp.where(sublane == k, reduced[k], out)
        tiles[b] = out
        if b < n // 8 - 1:
            solved = list(reduced)
            for k in range(7, -1, -1):
                solved[k] = solved[k] * p[k]
                for m in range(k):
                    solved[m] = solved[m] - low[k, m] * solved[k]
            for v in range(b + 1, n // 8):
                old = tiles[v]
                new = old
                for k in range(8):
                    new = new - jnp.broadcast_to(old[:, 8 * b + k : 8 * b + k + 1], full) * solved[k]
                tiles[v] = new
    return jnp.concatenate(tiles, axis=0)[:, n:]


def subspace_kernel(gram_ref, start_ref, out_ref, image_ref, work_ref, block_ref):
    size = start_ref.shape[1]
    out_ref[...] = start_ref[...]
    blocks = size // OUTER

    def iteration(step, carry):
        image_ref[...] = dot(gram_ref[...], out_ref[...], 1, 0)
        image = image_ref[...]
        work_ref[:, :size] = dot(image, image, 0, 0)
        lane = lax.broadcasted_iota(jnp.int32, (size, size), 1)
        sub = lax.broadcasted_iota(jnp.int32, (size, size), 0)
        work_ref[:, size:] = jnp.where(lane == sub, 1.0, 0.0).astype(jnp.float32)
        block_ref[...] = work_ref[:OUTER, :OUTER]

        def outer(o, carry):
            inverse = block_inverse(block_ref[...])
            for s in range(blocks):

                @pl.when(o == s)
                def _():
                    low, high = s * OUTER, (s + 1) * OUTER
                    rows = dot(inverse, work_ref[low:high, :], 1, 0)
                    work_ref[low:high, :] = rows
                    if s < blocks - 1:
                        work_ref[high:, :] -= dot(rows[:, high:size], rows, 0, 0)
                        block_ref[...] = work_ref[high : high + OUTER, high : high + OUTER]

            return carry

        lax.fori_loop(0, blocks, outer, 0)
        scale = jnp.where(step == ITERS - 1, math.sqrt(gram_ref.shape[0]), 1.0).astype(jnp.float32)
        out_ref[...] = dot(image_ref[...], work_ref[:, size:], 1, 1) * scale
        return carry

    lax.fori_loop(0, ITERS, iteration, 0)


def subspace(gram, start):
    length, size = start.shape
    return pl.pallas_call(
        subspace_kernel,
        out_shape=jax.ShapeDtypeStruct((length, size), jnp.float32),
        in_specs=[pl.BlockSpec(memory_space=pltpu.VMEM)] * 2,
        out_specs=pl.BlockSpec(memory_space=pltpu.VMEM),
        scratch_shapes=[
            pltpu.VMEM((length, size), jnp.float32),
            pltpu.VMEM((size, 2 * size), jnp.float32),
            pltpu.VMEM((OUTER, OUTER), jnp.float32),
        ],
        compiler_params=pltpu.CompilerParams(vmem_limit_bytes=40 * 2**20),
        name="subspace",
    )(gram, start)


def shards(cube, mode3_factor, mode2_factor, start_basis):
    rows, width2, width3 = cube.shape
    rank = mode3_factor.shape[1]
    n_depth = lax.axis_size("depth")
    flat = cube.reshape(rows * width2, width3)
    rank3 = rank // n_depth
    middle = lax.psum_scatter(
        lax.dot_general(
            mode3_factor, flat, (((0,), (1,)), ((), ())), preferred_element_type=jnp.float32
        ).astype(jnp.bfloat16),
        "depth",
        scatter_dimension=0,
        tiled=True,
    )
    middle = middle.reshape(rank3, rows, width2)
    middle = lax.all_to_all(middle, "col", 0, 2, tiled=True)
    factor2 = lax.all_gather(mode2_factor, "col", axis=0, tiled=True)
    core = jnp.einsum("tij,jr->tri", middle, factor2, preferred_element_type=jnp.float32)
    core = core.astype(jnp.bfloat16)
    core = lax.all_to_all(core, "row", 1, 2, tiled=True)
    core = core.reshape(-1, core.shape[2])
    gram = lax.psum(dot(core, core, 0, 0, None), ("row", "col", "depth"))
    start = lax.all_gather(start_basis, "row", axis=0, tiled=True)
    basis = subspace(gram, start)
    return lax.dynamic_slice_in_dim(basis, lax.axis_index("row") * rows, rows, 0)


def solution(mesh):
    in_specs = (P("row", "col", "depth"), P("depth", None), P("col", None), P("row", None))
    out_specs = P("row", None)
    return jax.shard_map(shards, mesh=mesh, in_specs=in_specs, out_specs=out_specs, check_vma=False)
```

time: 786 us -> 479 us (0.61)
  other arithmetic: 218 us -> 0 us
  waiting for transfers between devices: 429 us -> 221 us
  blocking collectives: 9.81 us -> 139 us
  Pallas kernels: 0 us -> 58.5 us
  local copies, waits for them, and re-layouts: 57.9 us -> 26.7 us
  matrix products: 43.3 us -> 14 us
    another operation x36 -> x0, other arithmetic: 218 us -> none  [the longest x27 139 us: orthonormal(): lower = jnp.linalg.cholesky(cross)]
    reduce_scatter x2 -> x1, waiting for transfers between devices: 270 us -> 102 us  [shards(): lax.psum_scatter(lax.dot_general(mode3_factor, flat, (((0,), (1,)), ((),...]
    all_gather x1 -> x2, blocking collectives: 9.81 us -> 110 us  [the longest x1 101 us: shards(): factor2 = lax.all_gather(mode2_factor, 'col', axis=0, tiled=True)]
    all_gather x2 -> x0, waiting for transfers between devices: 68.6 us -> none  [the longest x1 55.2 us: shards(): lax.all_gather(core, 'row', axis=1, tiled=True)]
    pallas_call x0 -> x1, Pallas kernels: none -> 58.5 us  [subspace(): pl.pallas_call(subspace_kernel, out_shape=jax.ShapeDtypeStruct((length, s...]
    all_to_all x0 -> x1, blocking collectives: none -> 29 us  [shards(): core = lax.all_to_all(core, 'row', 1, 2, tiled=True)]
    psum x1, waiting for transfers between devices: 90.2 us -> 119 us  [shards(): gram = lax.psum(dot(core, core, 0, 0, None), ('row', 'col', 'depth'))]
    dot_general x11 -> x3, matrix products: 35.7 us -> 14 us  [the longest x1 9.02 us: shards(): lax.dot_general(mode3_factor, flat, (((0,), (1,)), ((), ())), preferred_e...]
  transfers between devices with their start and end apart: 5 -> 3, of which waited for: 5 -> 2; matrix products, arithmetic and copies ran while one was open for 0% -> 0% of each run, Pallas kernels for 0% -> 0%
where the time goes in v1:
time: 479 us; the launch traced here: 478 us
  waiting for transfers between devices  221 us (46%)
  blocking collectives  139 us (29%)
  Pallas kernels  58.5 us (12%)
  local copies, waits for them, and re-layouts  26.7 us (6%)
  matrix products  14 us (3%)
  between operations  13.5 us (3%)
  starting transfers between devices  4.79 us (1%)
    psum x1, waiting for transfers between devices, shards(): gram = lax.psum(dot(core, core, 0, 0, None), ('row', 'col', 'depth'))  119 us
    reduce_scatter x1, waiting for transfers between devices, shards(): lax.psum_scatter(lax.dot_general(mode3_factor, flat, (((0,), (1,)), ((),...  102 us
    all_gather x1, blocking collectives, shards(): factor2 = lax.all_gather(mode2_factor, 'col', axis=0, tiled=True)  101 us
    pallas_call x1, Pallas kernels, subspace(): pl.pallas_call(subspace_kernel, out_shape=jax.ShapeDtypeStruct((length, s...  58.5 us
    all_to_all x1, blocking collectives, shards(): core = lax.all_to_all(core, 'row', 1, 2, tiled=True)  29 us
  transfers between devices with their start and end apart: 3, of which 2 were waited for; matrix products, arithmetic and copies ran while one was open for 0% of the time, Pallas kernels for 0%

profile of v1, /device:TPU:0, one launch (start us, length us, event | category | flops | bytes accessed | tf_op | source)
XLA Modules:
  0.0 478.0 jit_solution(6806389238068193155)
XLA Ops:
  6.5 0.0 copy-start
  6.5 0.9 copy-done
  7.4 9.0 %convolution_convert_fusion = bf16[256,16384]{1,0:T(8,128)(2,1)} fusion(bf16[256,256]{1,0:T(8,128)(2,1)S(1)} %copy-done, bf16[16384,256]{1,0:T(8,128)(2,1)} %bitcast.24), kind=kOutput, calls=%fused_computation | convolution fusion | flops 2151677952 | bytes 16908288 | tf_op jit(solution)/shard_map/dot_general | solution.py:131
  16.5 0.0 reduce-scatter.2.cloned.1.call-update
  16.5 102.1 %reduce-scatter.2.cloned.1.call-done = bf16[128,16384]{1,0:T(8,128)(2,1)} async-done(((bf16[256,16384]{1,0:T(8,128)(2,1)}), bf16[128,16384]{1,0:T(8,128)(2,1)}) %reduce-scatter.2.cloned.1.call-update) | async-done | bytes 4194320 | tf_op jit(solution)/shard_map/reduce_scatter | solution.py:130
  118.6 6.4 %copy.22 = bf16[128,16384]{0,1:T(8,128)(2,1)} copy(bf16[128,16384]{1,0:T(8,128)(2,1)} %reduce-scatter.2.cloned.1.call-done) | data formatting | bytes 8388608 | tf_op jit(solution)/shard_map/reduce_scatter | solution.py:130
  124.9 7.4 %copy.23 = bf16[128,256,64]{1,2,0:T(8,128)(2,1)} copy(bf16[128,256,64]{0,2,1:T(8,128)(2,1)} %bitcast.23) | data formatting | bytes 8388608 | tf_op jit(solution)/shard_map/reshape | solution.py:138
  132.3 4.7 all-to-all-start
  137.1 0.0 all-reduce.2.cloned.1.call-start
  137.1 100.9 %all_gather.6 = bf16[512,256]{1,0:T(8,128)(2,1)S(1)} all-gather(bf16[64,256]{1,0:T(8,128)(2,1)S(1)} %copy-done.3), channel_id=1, replica_groups=mesh['row'=2,'col'=8,'depth'=2] {'col'}, dimensions={0}, use_global_device_ids=true | all-gather | bytes 294912 | tf_op jit(solution)/shard_map/all_gather | solution.py:140
  238.0 0.0 all-to-all-done
  238.0 2.5 copy.24
  240.5 2.7 convert_bitcast_fusion
  243.2 3.3 copy.26
  246.5 29.0 %all_to_all.33 = bf16[16,256,256]{2,0,1:T(8,128)(2,1)} all-to-all(bf16[16,256,256]{2,0,1:T(8,128)(2,1)S(1)} %copy.26), channel_id=1, replica_groups=mesh['row'=2,'col'=8,'depth'=2] {'row'}, dimensions={1} | all-to-all | bytes 4194304 | tf_op jit(solution)/shard_map/all_to_all | solution.py:143
  275.5 4.2 copy.27
  279.8 0.0 copy-start.2
  279.8 2.3 fusion
  282.1 0.0 all-reduce.2.cloned.1.call-update
  282.2 9.4 %all_gather.7.start_ref = f32[512,256]{1,0:T(8,128)S(1)} all-gather(f32[256,256]{1,0:T(8,128)S(1)} %copy-done.2), channel_id=1, replica_groups=mesh['row'=2,'col'=8,'depth'=2] {'row'}, dimensions={0}, use_global_device_ids=true | all-gather | bytes 786432 | tf_op jit(solution)/shard_map/all_gather | solution.py:146
  291.6 119.1 %all-reduce.2.cloned.1.call-done.gram_ref = f32[512,512]{1,0:T(8,128)} async-done(((f32[512,512]{1,0:T(8,128)}), f32[512,512]{1,0:T(8,128)}) %all-reduce.2.cloned.1.call-update) | async-done | bytes 1048592 | tf_op jit(solution)/shard_map/psum | solution.py:145
  410.7 1.2 copy-done.1
  411.9 58.5 %subspace.1 = f32[512,256]{1,0:T(8,128)S(1)} custom-call(f32[512,512]{1,0:T(8,128)S(1)} %copy-done.1, f32[512,256]{1,0:T(8,128)S(1)} %all_gather.7.start_ref), custom_call_target="tpu_custom_call" | custom-call | tf_op jit(solution)/shard_map/subspace/pallas_call | solution.py:109
  470.5 0.7 constant_dynamic-slice_fusion
  (5 shorter events, 0.0 us)
Async XLA Ops:
  6.5 0.9 copy-start
  6.5 112.0 %reduce-scatter.2.cloned.1.call-start = ((), (), s32[]{:S(2)}) async-start(), calls=%async_computation.3 | async-start | bytes 12582912 | tf_op jit(solution)/shard_map/reduce_scatter | solution.py:130
  132.3 4.8 %copy-start.3 = (bf16[64,256]{1,0:T(8,128)(2,1)S(1)}, bf16[64,256]{1,0:T(8,128)(2,1)}, u32[]{:S(2)}) copy-start(bf16[64,256]{1,0:T(8,128)(2,1)} %param.6) | copy-start | bytes 98308
  132.3 105.7 %all-to-all-start = ((bf16[128,256,64]{1,2,0:T(8,128)(2,1)}), bf16[128,256,64]{1,2,0:T(8,128)(2,1)}, u32[]{:S(2)}, u32[]{:S(2)}) async-start(bf16[128,256,64]{1,2,0:T(8,128)(2,1)} %copy.23), calls=%async_computation.1 | async-start | bytes 8388608 | tf_op jit(solution)/shard_map/all_to_all | solution.py:139
  137.1 273.6 %all-reduce.2.cloned.1.call-start = ((), (), s32[]{:S(2)}) async-start(), calls=%async_computation.4 | async-start | bytes 2097152 | tf_op jit(solution)/shard_map/psum | solution.py:145
  279.8 2.4 copy-start.2
  410.7 1.2 copy-start.1
Sparse Core Ops, SparseCore 0:
  16.6 101.9 reduce-scatter.1
  282.3 128.3 all-reduce.1

commit v2 on v1

--- a/solution.py
+++ b/solution.py
@@ -121,7 +121,236 @@
     )(gram, start)
 
 
-def shards(cube, mode3_factor, mode2_factor, start_basis):
+CHUNKS = 4
+MESH = pl.DeviceIdType.MESH
+
+
+def exchange_kernel(
+    sizes, cube_ref, m3_ref, m2_ref, start_ref, gram_out, start_out,
+    flat, outgoing, from_depth, middle, gathered, m2_all, m2_t, core, pairs, gram, start_all,
+    from_core, part, from_group, reduced, total,
+    x_send, x_recv, z_send, z_recv, y_send, y_recv, m_send, m_recv, s_send, s_recv,
+    c_send, c_recv, g_send, g_recv,
+):
+    n_row, n_col, n_depth = sizes
+    width2, rows, width3 = cube_ref.shape
+    per = middle.shape[2]
+    count = n_depth * n_col * per
+    rank2 = m2_ref.shape[1]
+    half2 = rank2 // n_row
+    row, col, depth = lax.axis_index("row"), lax.axis_index("col"), lax.axis_index("depth")
+    n_z = n_col // 2
+    z, parity = col // 2, col % 2
+    other_row, other_depth = 1 - row, 1 - depth
+
+    barrier = pltpu.get_barrier_semaphore()
+    others = 0
+    for dr in range(n_row):
+        for dc in range(n_col):
+            for dd in range(n_depth):
+                if dr or dc or dd:
+                    target = ((row + dr) % n_row, (col + dc) % n_col, (depth + dd) % n_depth)
+                    pl.semaphore_signal(barrier, inc=1, device_id=target, device_id_type=MESH)
+                    others += 1
+    pl.semaphore_wait(barrier, others)
+
+    started = []
+
+    def send(src, dst, send_sem, recv_sem, target):
+        copy = pltpu.make_async_remote_copy(
+            src_ref=src, dst_ref=dst, send_sem=send_sem, recv_sem=recv_sem,
+            device_id=target, device_id_type=MESH,
+        )
+        copy.start()
+        started.append(copy)
+        return copy
+
+    own2 = pl.ds(pl.multiple_of(col * width2, width2), width2)
+    m_copies = [
+        send(m2_ref, m2_all.at[own2, :], m_send.at[o], m_recv.at[o], (row, (col + o) % n_col, depth))
+        for o in range(1, n_col)
+    ]
+    own_rows = pl.ds(pl.multiple_of(row * rows, rows), rows)
+    s_copy = send(start_ref, start_all.at[own_rows, :], s_send, s_recv, (other_row, col, depth))
+    m2_all[own2, :] = m2_ref[...]
+    start_all[own_rows, :] = start_ref[...]
+    gram[...] = jnp.zeros_like(gram)
+    x_copies, z_copies, y_copies = {}, {}, {}
+
+    def first(q):
+        def multiply(j, carry):
+            tile = dot(m3_ref[q], cube_ref[j], 1, 1, None)
+            for h in range(rows // 128):
+                flat[h, pl.ds(j, count, stride=width2), :] = tile[:, h * 128 : h * 128 + 128]
+            return carry
+
+        lax.fori_loop(0, width2, multiply, 0, unroll=4)
+        for d in range(n_depth):
+
+            def store(t, carry):
+                at = pl.ds(pl.multiple_of((d * n_col * per + t) * width2, width2), width2)
+                for h in range(rows // 128):
+                    outgoing[q, d, t, :, h * 128 : h * 128 + 128] = flat[h, at, :].astype(jnp.bfloat16)
+                return carry
+
+            lax.fori_loop(0, n_col * per, store, 0)
+        x_copies[q] = send(
+            outgoing.at[q, other_depth], from_depth.at[q], x_send.at[q], x_recv.at[q],
+            (row, col, other_depth),
+        )
+
+    def second(q):
+        x_copies[q].wait_recv()
+
+        for c in range(n_col):
+            for t in range(per):
+                a = outgoing[q, depth, c * per + t].astype(jnp.float32)
+                b = from_depth[q, c * per + t].astype(jnp.float32)
+                middle[q, c, t] = (a + b).astype(jnp.bfloat16)
+        z_copies[q] = []
+        for o in range(1, n_col):
+            to = (col + o) % n_col
+            z_copies[q].append(
+                send(
+                    middle.at[q, to], gathered.at[q, :, own2, :], z_send.at[q, o], z_recv.at[q, o],
+                    (row, to, depth),
+                )
+            )
+        gathered[q, :, own2, :] = middle[q, col]
+
+    def third(q):
+        if q == 0:
+            for copy in m_copies:
+                copy.wait_recv()
+            m2_t[...] = m2_all[...].astype(jnp.float32).T.astype(jnp.bfloat16)
+        for copy in z_copies[q]:
+            copy.wait_recv()
+
+        def multiply(t, carry):
+            core[q, t] = dot(m2_t[...], gathered[q, t], 1, 0, None).astype(jnp.bfloat16)
+            return carry
+
+        lax.fori_loop(0, per, multiply, 0)
+        mine = pl.ds(pl.multiple_of(row * half2, half2), half2)
+        theirs = pl.ds(pl.multiple_of(other_row * half2, half2), half2)
+        lanes = pl.ds(pl.multiple_of(row * rows, rows), rows)
+        y_copies[q] = send(
+            core.at[q, :, theirs, :], pairs.at[q, :, :, lanes], y_send.at[q], y_recv.at[q],
+            (other_row, col, depth),
+        )
+        pairs[q, :, :, lanes] = core[q, :, mine, :]
+
+    def fourth(q):
+        y_copies[q].wait_recv()
+        x = pairs[q].reshape(per * half2, n_row * rows)
+        gram[...] += dot(x, x, 0, 0, None)
+
+    stages = [first, second, third, fourth]
+    for wave in range(CHUNKS + 3):
+        for stage in range(4):
+            if 0 <= wave - stage < CHUNKS:
+                stages[stage](wave - stage)
+
+    length = gram.shape[0]
+    half = length // 2
+    piece = half // (n_row * n_z * n_depth)
+
+    def group(r, zz, d):
+        return (r * n_z + zz) * n_depth + d
+
+    keep = pl.ds(pl.multiple_of(parity * half, half), half)
+    give = pl.ds(pl.multiple_of((1 - parity) * half, half), half)
+    partner = (row, z * 2 + 1 - parity, depth)
+    copy = send(gram.at[give, :], from_core, c_send.at[0], c_recv.at[0], partner)
+    copy.wait_recv()
+    part[...] = gram[keep, :] + from_core[...]
+    offsets = [
+        (dr, dz, dd)
+        for dz in range(n_z) for dr in range(n_row) for dd in range(n_depth) if dr or dz or dd
+    ]
+    me = group(row, z, depth)
+    copies = []
+    for k, (dr, dz, dd) in enumerate(offsets):
+        r, zz, d = (row + dr) % n_row, (z + dz) % n_z, (depth + dd) % n_depth
+        at = pl.ds(pl.multiple_of(group(r, zz, d) * piece, piece), piece)
+        copies.append(
+            send(part.at[at, :], from_group.at[k], g_send.at[0, k], g_recv.at[0, k], (r, zz * 2 + parity, d))
+        )
+    value = part[pl.ds(pl.multiple_of(me * piece, piece), piece), :]
+    for k, copy in enumerate(copies):
+        copy.wait_recv()
+        value = value + from_group[k]
+    reduced[...] = value
+    here = pl.ds(pl.multiple_of(parity * half + me * piece, piece), piece)
+    copies = []
+    for k, (dr, dz, dd) in enumerate(offsets):
+        r, zz, d = (row + dr) % n_row, (z + dz) % n_z, (depth + dd) % n_depth
+        copies.append(
+            send(reduced, total.at[here, :], g_send.at[1, k], g_recv.at[1, k], (r, zz * 2 + parity, d))
+        )
+    total[here, :] = value
+    for copy in copies:
+        copy.wait_recv()
+    copy = send(total.at[keep, :], total.at[keep, :], c_send.at[1], c_recv.at[1], partner)
+    s_copy.wait_recv()
+    start_out[...] = start_all[...]
+    copy.wait_recv()
+    gram_out[...] = total[...]
+    for copy in started:
+        copy.wait_send()
+
+
+def exchange(sizes, cube, mode3_factor, mode2_factor, start_basis):
+    n_row, n_col, n_depth = sizes
+    rows, width2, width3 = cube.shape
+    rank3, rank2 = mode3_factor.shape[1], mode2_factor.shape[1]
+    per = rank3 // (n_depth * n_col * CHUNKS)
+    cube_t = jnp.swapaxes(cube, 0, 1)
+    m3 = mode3_factor.T.reshape(n_depth, n_col, CHUNKS, per, width3)
+    m3 = m3.transpose(2, 0, 1, 3, 4).reshape(CHUNKS, n_depth * n_col * per, width3)
+    length, half2 = n_row * rows, rank2 // n_row
+    count = n_depth * n_col * per
+    group = n_row * n_col // 2 * n_depth
+    piece = length // 2 // group
+    bf16, f32, dma = jnp.bfloat16, jnp.float32, pltpu.SemaphoreType.DMA
+    vmem = pl.BlockSpec(memory_space=pltpu.VMEM)
+    return pl.pallas_call(
+        functools.partial(exchange_kernel, sizes),
+        out_shape=[
+            jax.ShapeDtypeStruct((length, length), f32),
+            jax.ShapeDtypeStruct((length, start_basis.shape[1]), f32),
+        ],
+        in_specs=[vmem] * 4,
+        out_specs=[vmem] * 2,
+        scratch_shapes=[
+            pltpu.VMEM((rows // 128, count * width2, 128), f32),
+            pltpu.VMEM((CHUNKS, n_depth, n_col * per, width2, rows), bf16),
+            pltpu.VMEM((CHUNKS, n_col * per, width2, rows), bf16),
+            pltpu.VMEM((CHUNKS, n_col, per, width2, rows), bf16),
+            pltpu.VMEM((CHUNKS, per, n_col * width2, rows), bf16),
+            pltpu.VMEM((n_col * width2, rank2), bf16),
+            pltpu.VMEM((rank2, n_col * width2), bf16),
+            pltpu.VMEM((CHUNKS, per, rank2, rows), bf16),
+            pltpu.VMEM((CHUNKS, per, half2, length), bf16),
+            pltpu.VMEM((length, length), f32),
+            pltpu.VMEM((length, start_basis.shape[1]), f32),
+            pltpu.VMEM((length // 2, length), f32),
+            pltpu.VMEM((length // 2, length), f32),
+            pltpu.VMEM((group - 1, piece, length), f32),
+            pltpu.VMEM((piece, length), f32),
+            pltpu.VMEM((length, length), f32),
+            dma((CHUNKS,)), dma((CHUNKS,)), dma((CHUNKS, n_col)), dma((CHUNKS, n_col)),
+            dma((CHUNKS,)), dma((CHUNKS,)), dma((n_col,)), dma((n_col,)), dma, dma,
+            dma((2,)), dma((2,)), dma((2, group)), dma((2, group)),
+        ],
+        compiler_params=pltpu.CompilerParams(
+            collective_id=0, has_side_effects=True, vmem_limit_bytes=60 * 2**20
+        ),
+        name="exchange",
+    )(cube_t, m3, mode2_factor, start_basis)
+
+
+def collectives(cube, mode3_factor, mode2_factor, start_basis):
     rows, width2, width3 = cube.shape
     rank = mode3_factor.shape[1]
     n_depth = lax.axis_size("depth")
@@ -144,6 +373,16 @@
     core = core.reshape(-1, core.shape[2])
     gram = lax.psum(dot(core, core, 0, 0, None), ("row", "col", "depth"))
     start = lax.all_gather(start_basis, "row", axis=0, tiled=True)
+    return gram, start
+
+
+def shards(cube, mode3_factor, mode2_factor, start_basis):
+    rows = cube.shape[0]
+    sizes = tuple(lax.axis_size(name) for name in ("row", "col", "depth"))
+    if sizes[0] == 2 and sizes[2] == 2 and rows % 128 == 0 and rows * 2 % (16 * sizes[1] * 4) == 0:
+        gram, start = exchange(sizes, cube, mode3_factor, mode2_factor, start_basis)
+    else:
+        gram, start = collectives(cube, mode3_factor, mode2_factor, start_basis)
     basis = subspace(gram, start)
     return lax.dynamic_slice_in_dim(basis, lax.axis_index("row") * rows, rows, 0)
 

time: 479 us -> 243 us (0.51)
  waiting for transfers between devices: 221 us -> 0 us
  Pallas kernels: 58.5 us -> 227 us
  blocking collectives: 139 us -> 0 us
  matrix products: 14 us -> 0 us
  between operations: 13.5 us -> 0.05 us
  local copies, waits for them, and re-layouts: 26.7 us -> 15.3 us
  starting transfers between devices: 4.79 us -> 0 us
    pallas_call x0 -> x1, Pallas kernels: none -> 168 us  [exchange(): pl.pallas_call(functools.partial(exchange_kernel, sizes), out_shape=[jax....]
    psum x1 -> x0, waiting for transfers between devices: 119 us -> none  [shards(): gram = lax.psum(dot(core, core, 0, 0, None), ('row', 'col', 'depth'))]
    all_gather x2 -> x0, blocking collectives: 110 us -> none  [the longest x1 101 us: shards(): factor2 = lax.all_gather(mode2_factor, 'col', axis=0, tiled=True)]
    reduce_scatter x1 -> x0, waiting for transfers between devices: 102 us -> none  [shards(): lax.psum_scatter(lax.dot_general(mode3_factor, flat, (((0,), (1,)), ((),...]
    all_to_all x1 -> x0, blocking collectives: 29 us -> none  [shards(): core = lax.all_to_all(core, 'row', 1, 2, tiled=True)]
    dot_general x3 -> x0, matrix products: 14 us -> none  [the longest x1 9.02 us: shards(): lax.dot_general(mode3_factor, flat, (((0,), (1,)), ((), ())), preferred_e...]
    unnamed x8 -> x7, local copies, waits for them, and re-layouts: 2.14 us -> 13.7 us
    all_to_all x2 -> x0, local copies, waits for them, and re-layouts: 6.74 us -> none  [the longest x1 4.24 us: shards(): core = lax.all_to_all(core, 'row', 1, 2, tiled=True)]
  transfers between devices with their start and end apart: 3 -> 0, of which waited for: 2 -> 0; matrix products, arithmetic and copies ran while one was open for 0% -> 0% of each run, Pallas kernels for 0% -> 0%
where the time goes in v2:
time: 243 us; the launch traced here: 242 us
  Pallas kernels  227 us (93%)
  local copies, waits for them, and re-layouts  15.3 us (6%)
    pallas_call x1, Pallas kernels, exchange(): pl.pallas_call(functools.partial(exchange_kernel, sizes), out_shape=[jax....  168 us
    pallas_call x1, Pallas kernels, subspace(): pl.pallas_call(subspace_kernel, out_shape=jax.ShapeDtypeStruct((length, s...  58.5 us
    unnamed x7, local copies, waits for them, and re-layouts  13.7 us

profile of v2, /device:TPU:0, one launch (start us, length us, event | category | flops | bytes accessed | tf_op | source)
XLA Modules:
  0.0 242.4 jit_solution(4434214566203593970)
XLA Ops:
  0.0 0.0 copy-start.2
  0.0 11.4 %copy.11 = bf16[256,64,256]{2,0,1:T(8,128)(2,1)} copy(bf16[256,64,256]{2,1,0:T(8,128)(2,1)} %param.4) | data formatting | bytes 16777216 | tf_op args[0]
  11.4 0.0 copy-done.2
  11.4 0.1 copy.8
  11.6 0.7 reshape.7.m3_ref
  12.3 168.5 %exchange.1 = (f32[512,512]{1,0:T(8,128)}, f32[512,256]{1,0:T(8,128)}) custom-call(bf16[64,256,256]{2,1,0:T(8,128)(2,1)} %bitcast.5, bf16[4,64,256]{2,1,0:T(8,128)(2,1)} %reshape.7.m3_ref, bf16[64,256]{1,0:T(8,128)(2,1)} %m2_ref.1, f32[256,256]{1,0:T(8,128)} %start_ref.1), custom_call_target="tpu_custom_call" | custom-call | tf_op jit(solution)/shard_map/exchange/pallas_call | solution.py:317
  180.8 0.0 copy-start
  180.8 1.2 copy-done
  182.0 0.0 copy-start.1
  182.0 1.0 copy-done.1
  183.1 58.5 %subspace.1 = f32[512,256]{1,0:T(8,128)S(1)} custom-call(f32[512,512]{1,0:T(8,128)S(1)} %copy-done, f32[512,256]{1,0:T(8,128)S(1)} %copy-done.1), custom_call_target="tpu_custom_call" | custom-call | tf_op jit(solution)/shard_map/subspace/pallas_call | solution.py:109
  241.6 0.7 constant_dynamic-slice_fusion
  (2 shorter events, 0.1 us)
Async XLA Ops:
  0.0 11.4 %copy-start.2 = (bf16[256,256]{1,0:T(8,128)(2,1)S(1)}, bf16[256,256]{1,0:T(8,128)(2,1)}, u32[]{:S(2)}) copy-start(bf16[256,256]{1,0:T(8,128)(2,1)} %param.5) | copy-start | bytes 393220
  180.8 1.2 copy-start
  182.0 1.0 copy-start.1

commit v3 on v2

--- a/solution.py
+++ b/solution.py
@@ -9,7 +9,7 @@
 from jax.sharding import PartitionSpec as P
 
 ITERS = 4
-OUTER = 64
+OUTER = 128
 HIGHEST = lax.Precision.HIGHEST
 
 
@@ -121,7 +121,7 @@
     )(gram, start)
 
 
-CHUNKS = 4
+CHUNKS = 8
 MESH = pl.DeviceIdType.MESH
 
 
@@ -243,7 +243,10 @@
     def fourth(q):
         y_copies[q].wait_recv()
         x = pairs[q].reshape(per * half2, n_row * rows)
-        gram[...] += dot(x, x, 0, 0, None)
+        low, high = x[:, :rows], x[:, rows:]
+        gram[:rows, :] += dot(low, low, 0, 0, None)
+        gram[rows : 2 * rows, :] += dot(high, low, 0, 0, None)
+        gram[2 * rows :, :] += dot(high, high, 0, 0, None)
 
     stages = [first, second, third, fourth]
     for wave in range(CHUNKS + 3):
@@ -295,7 +298,11 @@
     s_copy.wait_recv()
     start_out[...] = start_all[...]
     copy.wait_recv()
-    gram_out[...] = total[...]
+    cross = total[rows : 2 * rows, :]
+    gram_out[:rows, :rows] = total[:rows, :]
+    gram_out[rows:, :rows] = cross
+    gram_out[:rows, rows:] = cross.T
+    gram_out[rows:, rows:] = total[2 * rows :, :]
     for copy in started:
         copy.wait_send()
 
@@ -309,9 +316,10 @@
     m3 = mode3_factor.T.reshape(n_depth, n_col, CHUNKS, per, width3)
     m3 = m3.transpose(2, 0, 1, 3, 4).reshape(CHUNKS, n_depth * n_col * per, width3)
     length, half2 = n_row * rows, rank2 // n_row
+    blocks = 3 * rows
     count = n_depth * n_col * per
     group = n_row * n_col // 2 * n_depth
-    piece = length // 2 // group
+    piece = blocks // 2 // group
     bf16, f32, dma = jnp.bfloat16, jnp.float32, pltpu.SemaphoreType.DMA
     vmem = pl.BlockSpec(memory_space=pltpu.VMEM)
     return pl.pallas_call(
@@ -332,13 +340,13 @@
             pltpu.VMEM((rank2, n_col * width2), bf16),
             pltpu.VMEM((CHUNKS, per, rank2, rows), bf16),
             pltpu.VMEM((CHUNKS, per, half2, length), bf16),
-            pltpu.VMEM((length, length), f32),
+            pltpu.VMEM((blocks, rows), f32),
             pltpu.VMEM((length, start_basis.shape[1]), f32),
-            pltpu.VMEM((length // 2, length), f32),
-            pltpu.VMEM((length // 2, length), f32),
-            pltpu.VMEM((group - 1, piece, length), f32),
-            pltpu.VMEM((piece, length), f32),
-            pltpu.VMEM((length, length), f32),
+            pltpu.VMEM((blocks // 2, rows), f32),
+            pltpu.VMEM((blocks // 2, rows), f32),
+            pltpu.VMEM((group - 1, piece, rows), f32),
+            pltpu.VMEM((piece, rows), f32),
+            pltpu.VMEM((blocks, rows), f32),
             dma((CHUNKS,)), dma((CHUNKS,)), dma((CHUNKS, n_col)), dma((CHUNKS, n_col)),
             dma((CHUNKS,)), dma((CHUNKS,)), dma((n_col,)), dma((n_col,)), dma, dma,
             dma((2,)), dma((2,)), dma((2, group)), dma((2, group)),
@@ -379,7 +387,7 @@
 def shards(cube, mode3_factor, mode2_factor, start_basis):
     rows = cube.shape[0]
     sizes = tuple(lax.axis_size(name) for name in ("row", "col", "depth"))
-    if sizes[0] == 2 and sizes[2] == 2 and rows % 128 == 0 and rows * 2 % (16 * sizes[1] * 4) == 0:
+    if sizes[0] == 2 and sizes[2] == 2 and rows % 128 == 0 and rows * 3 % (16 * sizes[1] * 2) == 0:
         gram, start = exchange(sizes, cube, mode3_factor, mode2_factor, start_basis)
     else:
         gram, start = collectives(cube, mode3_factor, mode2_factor, start_basis)

time: 243 us -> 220 us (0.905)
  Pallas kernels: 227 us -> 204 us
    pallas_call x1, Pallas kernels: 168 us -> 151 us  [exchange(): pl.pallas_call(functools.partial(exchange_kernel, sizes), out_shape=[jax....]
    pallas_call x1, Pallas kernels: 58.5 us -> 53.4 us  [subspace(): pl.pallas_call(subspace_kernel, out_shape=jax.ShapeDtypeStruct((length, s...]
where the time goes in v3:
time: 220 us
  Pallas kernels  204 us (93%)
  local copies, waits for them, and re-layouts  15.4 us (7%)
    pallas_call x1, Pallas kernels, exchange(): pl.pallas_call(functools.partial(exchange_kernel, sizes), out_shape=[jax....  151 us
    pallas_call x1, Pallas kernels, subspace(): pl.pallas_call(subspace_kernel, out_shape=jax.ShapeDtypeStruct((length, s...  53.4 us
    unnamed x7, local copies, waits for them, and re-layouts  13.7 us

profile of v3, /device:TPU:0, one launch (start us, length us, event | category | flops | bytes accessed | tf_op | source)
XLA Modules:
  0.0 219.6 jit_solution(16184378654478530022)
XLA Ops:
  0.0 0.0 copy-start.2
  0.0 11.4 %copy.11 = bf16[256,64,256]{2,0,1:T(8,128)(2,1)} copy(bf16[256,64,256]{2,1,0:T(8,128)(2,1)} %param.4) | data formatting | bytes 16777216 | tf_op args[0]
  11.4 0.0 copy-done.2
  11.4 0.1 copy.8
  11.5 0.1 reshape.6
  11.6 0.1 copy.9
  11.7 0.7 reshape.7.m3_ref
  12.4 150.8 %exchange.1 = (f32[512,512]{1,0:T(8,128)}, f32[512,256]{1,0:T(8,128)}) custom-call(bf16[64,256,256]{2,1,0:T(8,128)(2,1)} %bitcast.5, bf16[8,32,256]{2,1,0:T(8,128)(2,1)} %reshape.7.m3_ref, bf16[64,256]{1,0:T(8,128)(2,1)} %m2_ref.1, f32[256,256]{1,0:T(8,128)} %start_ref.1), custom_call_target="tpu_custom_call" | custom-call | tf_op jit(solution)/shard_map/exchange/pallas_call | solution.py:325
  163.2 0.0 copy-start
  163.2 1.2 copy-done
  164.4 0.0 copy-start.1
  164.4 1.0 copy-done.1
  165.4 53.4 %subspace.1 = f32[512,256]{1,0:T(8,128)S(1)} custom-call(f32[512,512]{1,0:T(8,128)S(1)} %copy-done, f32[512,256]{1,0:T(8,128)S(1)} %copy-done.1), custom_call_target="tpu_custom_call" | custom-call | tf_op jit(solution)/shard_map/subspace/pallas_call | solution.py:109
  218.9 0.7 constant_dynamic-slice_fusion
Async XLA Ops:
  0.0 11.4 %copy-start.2 = (bf16[256,256]{1,0:T(8,128)(2,1)S(1)}, bf16[256,256]{1,0:T(8,128)(2,1)}, u32[]{:S(2)}) copy-start(bf16[256,256]{1,0:T(8,128)(2,1)} %param.5) | copy-start | bytes 393220
  163.2 1.2 copy-start
  164.4 1.0 copy-start.1

commit v4 on v3

--- a/solution.py
+++ b/solution.py
@@ -88,10 +88,11 @@
                 @pl.when(o == s)
                 def _():
                     low, high = s * OUTER, (s + 1) * OUTER
-                    rows = dot(inverse, work_ref[low:high, :], 1, 0)
-                    work_ref[low:high, :] = rows
+                    rows = dot(inverse, work_ref[low:high, high : size + high], 1, 0)
+                    work_ref[low:high, high : size + high] = rows
                     if s < blocks - 1:
-                        work_ref[high:, :] -= dot(rows[:, high:size], rows, 0, 0)
+                        update = dot(rows[:, : size - high], rows, 0, 0)
+                        work_ref[high:, high : size + high] -= update
                         block_ref[...] = work_ref[high : high + OUTER, high : high + OUTER]
 
             return carry

time: 220 us -> 220 us (level)
  no operation moved by 1% of the time
where the time goes in v4:
time: 220 us; the launch traced here: 219 us
  Pallas kernels  204 us (93%)
  local copies, waits for them, and re-layouts  15.4 us (7%)
    pallas_call x1, Pallas kernels, exchange(): pl.pallas_call(functools.partial(exchange_kernel, sizes), out_shape=[jax....  151 us
    pallas_call x1, Pallas kernels, subspace(): pl.pallas_call(subspace_kernel, out_shape=jax.ShapeDtypeStruct((length, s...  52.8 us
    unnamed x7, local copies, waits for them, and re-layouts  13.7 us

profile of v4, /device:TPU:0, one launch (start us, length us, event | category | flops | bytes accessed | tf_op | source)
XLA Modules:
  0.0 219.0 jit_solution(1707182440020007316)
XLA Ops:
  0.0 0.0 copy-start.2
  0.0 11.4 %copy.11 = bf16[256,64,256]{2,0,1:T(8,128)(2,1)} copy(bf16[256,64,256]{2,1,0:T(8,128)(2,1)} %param.4) | data formatting | bytes 16777216 | tf_op args[0]
  11.4 0.0 copy-done.2
  11.4 0.1 copy.8
  11.5 0.1 reshape.6
  11.6 0.1 copy.9
  11.7 0.7 reshape.7.m3_ref
  12.4 150.8 %exchange.1 = (f32[512,512]{1,0:T(8,128)}, f32[512,256]{1,0:T(8,128)}) custom-call(bf16[64,256,256]{2,1,0:T(8,128)(2,1)} %bitcast.5, bf16[8,32,256]{2,1,0:T(8,128)(2,1)} %reshape.7.m3_ref, bf16[64,256]{1,0:T(8,128)(2,1)} %m2_ref.1, f32[256,256]{1,0:T(8,128)} %start_ref.1), custom_call_target="tpu_custom_call" | custom-call | tf_op jit(solution)/shard_map/exchange/pallas_call | solution.py:326
  163.2 0.0 copy-start
  163.2 1.2 copy-done
  164.4 0.0 copy-start.1
  164.4 1.0 copy-done.1
  165.4 52.8 %subspace.1 = f32[512,256]{1,0:T(8,128)S(1)} custom-call(f32[512,512]{1,0:T(8,128)S(1)} %copy-done, f32[512,256]{1,0:T(8,128)S(1)} %copy-done.1), custom_call_target="tpu_custom_call" | custom-call | tf_op jit(solution)/shard_map/subspace/pallas_call | solution.py:110
  218.3 0.7 constant_dynamic-slice_fusion
Async XLA Ops:
  0.0 11.4 %copy-start.2 = (bf16[256,256]{1,0:T(8,128)(2,1)S(1)}, bf16[256,256]{1,0:T(8,128)(2,1)}, u32[]{:S(2)}) copy-start(bf16[256,256]{1,0:T(8,128)(2,1)} %param.5) | copy-start | bytes 393220
  163.2 1.2 copy-start
  164.4 1.0 copy-start.1
